TPU v7x, 128 devices: a whole 4x4x4 slice. The times are simulated.
128 devices in a mesh: head: 4 (over x), inner: 8 (over y, z_hi), outer: 4 (over z_lo, core).
Axes of the slice: x: 4, y: 4, z: 4 (z_hi: 2, z_lo: 2; z = z_hi * 2 + z_lo), core: 2. Of those that a mesh axis runs over, the one named last changes fastest.
Arguments:
- query_rows: bfloat16 [32, 4, 128, 1024], P(('inner', 'outer'), 'head'), may hold values from -6 to 6
- key_rows: bfloat16 [32, 4, 128, 256], P(('inner', 'outer'), 'head'), may hold values from -6 to 6
- value_rows: bfloat16 [32, 4, 128, 256], P(('inner', 'outer'), 'head'), may hold values from -6 to 6
- out_grad: bfloat16 [32, 4, 128, 1024], P(('inner', 'outer'), 'head'), may hold values from -6 to 6
- lengths: int32 [4], replicated, may hold values from 1 to 12288, 16384 in all
Outputs:
- attended: bfloat16 [32, 4, 128, 1024], P(('inner', 'outer'), 'head')
- query_grad: bfloat16 [32, 4, 128, 1024], P(('inner', 'outer'), 'head')
- key_grad: bfloat16 [32, 4, 128, 256], P(('inner', 'outer'), 'head')
- value_grad: bfloat16 [32, 4, 128, 256], P(('inner', 'outer'), 'head')
Inputs may be any that keep to these rules, and one draw needn't show every extreme that they name: The 4 lengths sum to 16384; the largest is exactly 12288.
All inputs are finite; a program needn't handle non-finite values.
Results may differ from a plain program's by a relative error of at most 0.03.
Values may be sent and summed in bfloat16 or wider, within the bound.
No kernel may reach another device: no remote copies, remote signals or barrier semaphores. Data moves between devices by JAX's collectives and lax.ppermute only.
A program may use at most 64 MiB of HBM per device.

v0:
```python
import jax
import jax.numpy as jnp
from jax import lax
from jax.experimental import pallas as pl
from jax.experimental.pallas import tpu as pltpu
from jax.sharding import Mesh
from jax.sharding import PartitionSpec as P

HD = 128
NEG = -1.0e30
SCALE = HD ** -0.5
SC2 = SCALE * 1.4426950408889634
QT = 16
KP = 16
LIST = 160
TRIP = 8
WIDE = 1152
bf16, f32, i32 = jnp.bfloat16, jnp.float32, jnp.int32
VMEM = pl.BlockSpec(memory_space=pltpu.VMEM)
SMEM = pl.BlockSpec(memory_space=pltpu.SMEM)


def nt(a, b):
    return lax.dot_general(a, b, (((1,), (1,)), ((), ())), preferred_element_type=f32)


def nn(a, b):
    return jnp.dot(a, b, preferred_element_type=f32)


def row_tile(ref, n, first):
    n = jnp.minimum(n, QT - 1)
    return jnp.concatenate([ref[:, n, :, first + h * HD:first + (h + 1) * HD].reshape(64, HD) for h in range(4)], axis=0)


def head_tile(refs, n):
    n = jnp.minimum(n, QT - 1)
    return jnp.concatenate([ref[:, n].reshape(64, HD) for ref in refs], axis=0)


def key_tile(own_ref, oth_ref, p, first):
    parts = [own_ref[:, p, :, 512 + 256 * h + first:512 + 256 * h + first + HD].reshape(64, HD) for h in (0, 1)]
    parts += [oth_ref[:, p, :, 256 * h + first:256 * h + first + HD].reshape(64, HD) for h in (0, 1)]
    return jnp.concatenate(parts, axis=0)


def unpack(steps, kind, t):
    word = steps[kind, t]
    return lax.shift_right_logical(word, 8), word & 255


def mask_scores(s, n, p, pos_ref, kpos_ref, low):
    kpos = kpos_ref[...]
    kpos = jnp.concatenate([kpos, kpos], axis=1)
    first = p * 1024
    seen = (kpos <= pos_ref[n, 0:1, :] - first) & (kpos >= pos_ref[n, 1:2, :] - first)
    return jnp.where(seen, s, low)


def lanes_at(ref, p):
    return ref[:, pl.ds(pl.multiple_of(p * 256, 256), 256)]


def walk(count, score, soften, gather):
    score(0, 0)
    score(1, 1)
    trips = lax.shift_right_logical(count + 3, 2)

    @pl.loop(0, trips)
    def _(i):
        t = 4 * i
        for half in (0, 2):
            cur, nxt = half, 2 - half
            for k in (0, 1):
                score(t + half + 2 + k, nxt + k)
                soften(t + half + k, cur + k)
                gather(jnp.maximum(t + half - 2 + k, 0), nxt + k)

    last = jnp.maximum(4 * trips - 2, 0)
    gather(last, 2)
    gather(last + 1, 3)


def walk_two(count, soften, gather):
    for k in range(4):
        soften(k, k)

    @pl.loop(0, lax.shift_right_logical(count + 7, 3))
    def _(i):
        t = 8 * i
        for half in (0, 4):
            cur, nxt = half, 4 - half
            for k in range(4):
                gather(t + half + k, cur + k)
                soften(t + half + 4 + k, nxt + k)


def fwd_kernel(steps, pos_ref, kpos_ref, own_ref, oth_ref, ot_ref, st_ref, vt, m_s, l_s, acc, s_buf, p_buf, a_buf):
    @pl.loop(0, KP, unroll=4)
    def _(p):
        vt[:, pl.ds(pl.multiple_of(p * 256, 256), 256)] = key_tile(own_ref, oth_ref, p, HD).T

    m_s[...] = jnp.full_like(m_s, NEG)
    l_s[...] = jnp.zeros_like(l_s)
    acc[...] = jnp.zeros_like(acc)

    def run(kind):
        def score(t, buf):
            n, p = unpack(steps, kind, t)
            s = nt(key_tile(own_ref, oth_ref, p, 0), row_tile(own_ref, n, 0)) * SC2
            s_buf[buf] = mask_scores(s, n, p, pos_ref, kpos_ref, 2 * NEG) if kind else s

        def soften(t, buf):
            n, _ = unpack(steps, kind, t)
            s = s_buf[buf]
            old = m_s[n]
            new = jnp.maximum(old, jnp.max(s, axis=0, keepdims=True))
            w = jnp.exp2(s - new)
            alpha = jnp.exp2(old - new)
            m_s[n] = new
            l_s[n] = l_s[n] * alpha + jnp.sum(w, axis=0, keepdims=True)
            a_buf[buf] = alpha
            p_buf[buf] = w.astype(bf16)

        def gather(t, buf):
            n, p = unpack(steps, kind, t)
            acc[n] = acc[n] * a_buf[buf] + nn(lanes_at(vt, p), p_buf[buf])

        for buf in (2, 3):
            p_buf[buf] = jnp.zeros((256, 256), bf16)
            a_buf[buf] = jnp.ones((1, 256), f32)
        walk(steps[kind, LIST - 1], score, soften, gather)

    run(0)
    run(1)

    @pl.loop(0, QT, unroll=4)
    def _(n):
        o = acc[n]
        ot_ref[n] = o
        st_ref[n, 0:1, :] = m_s[n]
        st_ref[n, 1:2, :] = l_s[n]


def delta_kernel(st_ref, ot_ref, do0_ref, do1_ref, do2_ref, do3_ref, out_ref):
    refs = (do0_ref, do1_ref, do2_ref, do3_ref)

    @pl.loop(0, QT, unroll=4)
    def _(n):
        total = st_ref[n, 1:2, :]
        some = total > 0.0
        dots = jnp.sum(head_tile(refs, n).T.astype(f32) * ot_ref[n], axis=0, keepdims=True)
        out_ref[n, 0:1, :] = jnp.where(some, st_ref[n, 0:1, :] + jnp.log2(total), NEG)
        out_ref[n, 1:2, :] = jnp.where(some, dots / jnp.where(some, total, 1.0), 0.0)


def scale_kernel(st0_ref, st1_ref, st2_ref, st3_ref, st_ref, ot_ref, stat_ref, *out_refs):
    refs = (st0_ref, st1_ref, st2_ref, st3_ref)

    @pl.loop(0, QT, unroll=4)
    def _(n):
        parts = [refs[0][n]] + [pltpu.roll(refs[k][n], 64 * k, 1) for k in (1, 2, 3)]
        top = jnp.maximum(jnp.maximum(parts[0][0:1], parts[1][0:1]), jnp.maximum(parts[2][0:1], parts[3][0:1]))
        share = [jnp.exp2(part[0:1] - top) for part in parts]
        total = share[0] + share[1] + share[2] + share[3]
        lse = top + jnp.log2(total)
        stat_ref[n, 0:1, :] = lse
        stat_ref[n, 1:2, :] = sum(w * part[1:2] for w, part in zip(share, parts)) / total
        ob = (ot_ref[n] * jnp.exp2(st_ref[n, 0:1, :] - lse)).astype(bf16).T
        for h in range(4):
            out_refs[h][:, n] = ob[h * 64:(h + 1) * 64].reshape(4, 16, HD)
    stat_ref[QT, 0:1, :] = jnp.full((1, 256), -NEG, f32)
    stat_ref[QT, 1:2, :] = jnp.zeros((1, 256), f32)


def bwd_kernel(steps, pos_ref, kpos_ref, stat_ref, own_ref, oth_ref, do0_ref, do1_ref, do2_ref, do3_ref, kt, out_ref,
               oth_out_ref, dq, dk, dv, p_buf, ds_buf):
    do_refs = (do0_ref, do1_ref, do2_ref, do3_ref)

    dq[...] = jnp.zeros_like(dq)
    dk[...] = jnp.zeros_like(dk)
    dv[...] = jnp.zeros_like(dv)

    def run(kind):
        def soften(t, buf):
            n, p = unpack(steps, kind, t)
            s = nt(key_tile(own_ref, oth_ref, p, 0), row_tile(own_ref, n, 0)) * SC2
            if kind:
                s = mask_scores(s, n, p, pos_ref, kpos_ref, NEG)
            w = jnp.exp2(s - stat_ref[n, 0:1, :])
            dp = nt(key_tile(own_ref, oth_ref, p, HD), head_tile(do_refs, n))
            p_buf[buf] = w.astype(bf16)
            ds_buf[buf] = (w * (dp - stat_ref[n, 1:2, :])).astype(bf16)

        def gather(t, buf):
            n, p = unpack(steps, kind, t)
            ds = ds_buf[buf]
            dv[p] += nn(p_buf[buf], head_tile(do_refs, n))
            dk[p] += nn(ds, row_tile(own_ref, n, 0))
            dq[n] += nn(lanes_at(kt, p), ds)

        walk_two(steps[kind, LIST - 1], soften, gather)

    run(0)
    run(1)

    @pl.loop(0, QT, unroll=4)
    def _(n):
        qb = (dq[n] * SCALE).astype(bf16).T
        for h in range(4):
            out_ref[:, n, :, 640 + h * HD:768 + h * HD] = qb[h * 64:(h + 1) * 64].reshape(4, 16, HD)

    @pl.loop(0, KP, unroll=4)
    def _(p):
        for first, tile in ((0, (dk[p] * SCALE).astype(bf16)), (HD, dv[p].astype(bf16))):
            for h in (0, 1):
                at = 256 * h + first
                out_ref[:, p, :, at:at + HD] = tile[64 * h:64 * h + 64].reshape(4, 16, HD)
                oth_out_ref[:, p, :, at:at + HD] = tile[128 + 64 * h:192 + 64 * h].reshape(4, 16, HD)


def fwd(steps, pos, kpos, own, oth):
    return pl.pallas_call(
        fwd_kernel,
        in_specs=[SMEM] + [VMEM] * 4,
        out_specs=[VMEM, VMEM],
        scratch_shapes=[
            pltpu.VMEM((HD, KP * 256), bf16),
            pltpu.VMEM((QT + 1, 1, 256), f32), pltpu.VMEM((QT + 1, 1, 256), f32), pltpu.VMEM((QT + 1, HD, 256), f32),
            pltpu.VMEM((4, 256, 256), f32), pltpu.VMEM((4, 256, 256), bf16), pltpu.VMEM((4, 1, 256), f32),
        ],
        out_shape=[jax.ShapeDtypeStruct((QT, HD, 256), f32), jax.ShapeDtypeStruct((QT, 4, 256), f32)],
        compiler_params=pltpu.CompilerParams(vmem_limit_bytes=16 << 20),
        cost_estimate=pl.CostEstimate(flops=15 * 10 ** 9, bytes_accessed=8 << 20, transcendentals=0),
        name="fwd",
    )(steps, pos, kpos, own, oth)


def delta(st, ot, dos):
    return pl.pallas_call(
        delta_kernel, in_specs=[VMEM] * 6, out_specs=VMEM, out_shape=jax.ShapeDtypeStruct((QT, 2, 256), f32),
        compiler_params=pltpu.CompilerParams(vmem_limit_bytes=12 << 20), name="delta",
    )(st, ot, *dos)


def scale(sts, st, ot):
    return pl.pallas_call(
        scale_kernel, in_specs=[VMEM] * 6, out_specs=[VMEM] * 5,
        out_shape=[jax.ShapeDtypeStruct((QT + 1, 2, 256), f32)] + [jax.ShapeDtypeStruct((4, QT, 16, HD), bf16)] * 4,
        compiler_params=pltpu.CompilerParams(vmem_limit_bytes=12 << 20), name="scale",
    )(*sts, st, ot)


def turn_kernel(own_ref, oth_ref, kt):
    @pl.loop(0, KP, unroll=4)
    def _(p):
        kt[:, pl.ds(pl.multiple_of(p * 256, 256), 256)] = key_tile(own_ref, oth_ref, p, 0).T


def turn_keys(own, oth):
    return pl.pallas_call(
        turn_kernel, in_specs=[VMEM] * 2, out_specs=VMEM, out_shape=jax.ShapeDtypeStruct((HD, KP * 256), bf16),
        cost_estimate=pl.CostEstimate(flops=10 ** 9, bytes_accessed=2 << 20, transcendentals=0),
        compiler_params=pltpu.CompilerParams(vmem_limit_bytes=12 << 20), name="turn_keys",
    )(own, oth)


def bwd(steps, pos, kpos, stat, own, oth, dos, kt):
    return pl.pallas_call(
        bwd_kernel,
        in_specs=[SMEM] + [VMEM] * 10,
        out_specs=[VMEM] * 2,
        scratch_shapes=[
            pltpu.VMEM((QT + 1, HD, 256), f32), pltpu.VMEM((KP, 256, HD), f32), pltpu.VMEM((KP, 256, HD), f32),
            pltpu.VMEM((8, 256, 256), bf16), pltpu.VMEM((8, 256, 256), bf16),
        ],
        out_shape=[jax.ShapeDtypeStruct((4, QT, 16, WIDE), bf16), jax.ShapeDtypeStruct((4, KP, 16, 512), bf16)],
        compiler_params=pltpu.CompilerParams(vmem_limit_bytes=24 << 20),
        cost_estimate=pl.CostEstimate(flops=25 * 10 ** 9, bytes_accessed=8 << 20, transcendentals=0),
        name="bwd",
    )(steps, pos, kpos, stat, own, oth, *dos, kt)


def pack_kernel(q_hbm, k_hbm, v_hbm, do_hbm, out_hbm, q_ref, k_ref, v_ref, do_ref, out_ref, in_sem, out_sem):
    loads = [pltpu.make_async_copy(src, dst, in_sem.at[i])
             for i, (src, dst) in enumerate(((q_hbm, q_ref), (k_hbm, k_ref), (v_hbm, v_ref), (do_hbm, do_ref)))]
    for load in loads:
        load.start()
    for load in loads:
        load.wait()
    stores = []
    for j in range(4):
        for u in range(8):
            for g in range(2):
                at = u * 2 + g
                tokens = slice(16 * u, 16 * u + 16)
                for r in range(4):
                    head = 512 * g + HD * ((j - r) % 4)
                    out_ref[j, at, :, r * HD:r * HD + HD] = q_ref[tokens, head:head + HD]
                head = 512 * g + HD * j
                out_ref[j, at, :, 1024:1152] = do_ref[tokens, head:head + HD]
                for h in (0, 1):
                    rows = slice(32 * j + 16 * h, 32 * j + 16 * h + 16)
                    out_ref[j, at, :, 512 + 256 * h:640 + 256 * h] = k_ref[rows, HD * g:HD * g + HD]
                    out_ref[j, at, :, 640 + 256 * h:768 + 256 * h] = v_ref[rows, HD * g:HD * g + HD]
        stores.append(pltpu.make_async_copy(out_ref.at[j], out_hbm.at[j], out_sem.at[j]))
        stores[-1].start()
    for store in stores:
        store.wait()


def pack(q, k, v, do):
    any_spec = pl.BlockSpec(memory_space=pltpu.HBM)
    return pl.pallas_call(
        pack_kernel, in_specs=[any_spec] * 4, out_specs=any_spec,
        out_shape=jax.ShapeDtypeStruct((4, 16, 16, WIDE), bf16),
        scratch_shapes=[pltpu.VMEM((128, 1024), bf16), pltpu.VMEM((128, 256), bf16), pltpu.VMEM((128, 256), bf16),
                        pltpu.VMEM((128, 1024), bf16), pltpu.VMEM((4, 16, 16, WIDE), bf16), pltpu.SemaphoreType.DMA((4,)), pltpu.SemaphoreType.DMA((4,))],
        compiler_params=pltpu.CompilerParams(vmem_limit_bytes=60 << 20), name="pack",
    )(q, k, v, do)


def gather_kernel(oth_ref, o0_ref, o1_ref, o2_ref, o3_ref, out_ref, sum_ref):
    out_ref[...] = oth_ref[...]
    total = o0_ref[...].astype(f32) + o1_ref[...].astype(f32) + o2_ref[...].astype(f32) + o3_ref[...].astype(f32)
    sum_ref[...] = total.astype(bf16)


def gather_parts(oth, heads):
    return pl.pallas_call(
        gather_kernel, in_specs=[VMEM] * 5, out_specs=[VMEM] * 2,
        out_shape=[jax.ShapeDtypeStruct(oth.shape, bf16), jax.ShapeDtypeStruct(heads[0].shape, bf16)],
        compiler_params=pltpu.CompilerParams(vmem_limit_bytes=12 << 20), name="gather_parts",
    )(oth, *heads)


def add_kernel(own_ref, other_ref, head_ref, out_ref):
    out_ref[..., :512] = (own_ref[..., :512].astype(f32) + other_ref[...].astype(f32)).astype(bf16)
    out_ref[..., 512:] = head_ref[...]


def add_parts(out, other, head):
    block = lambda columns: pl.BlockSpec((1, KP, 16, columns), lambda i: (i, 0, 0, 0))
    return pl.pallas_call(
        add_kernel, grid=(4,), in_specs=[block(640), block(512), block(HD)], out_specs=block(640),
        out_shape=jax.ShapeDtypeStruct(out.shape, bf16), input_output_aliases={0: 0},
        compiler_params=pltpu.CompilerParams(vmem_limit_bytes=12 << 20), name="add_parts",
    )(out, other, head)


def sum_kernel(in_ref, at_ref, qg_ref, kg_ref, vg_ref):
    for u in range(8):
        for g in range(2):
            rows = slice(16 * u, 16 * u + 16)
            for h in range(4):
                cols = slice(512 * g + HD * h, 512 * g + HD * h + HD)
                at_ref[rows, cols] = in_ref[h * 16 + u * 2 + g, :, 512:640]
                first = [640 + HD * ((j - h) % 4) for j in range(4)]
                parts = [in_ref[j * 16 + u * 2 + g, :, first[j]:first[j] + HD].astype(f32) for j in range(4)]
                qg_ref[rows, cols] = (parts[0] + parts[1] + parts[2] + parts[3]).astype(bf16)
    for j in range(4):
        for g in range(2):
            for h in (0, 1):
                rows, cols = slice(32 * j + 16 * h, 32 * j + 16 * h + 16), slice(HD * g, HD * g + HD)
                both = sum(in_ref[j * 16 + u * 2 + g, :, 256 * h:256 * h + 256].astype(f32) for u in range(8))
                kg_ref[rows, cols] = both[:, :HD].astype(bf16)
                vg_ref[rows, cols] = both[:, HD:].astype(bf16)


def sum_pieces(pieces):
    big, small = jax.ShapeDtypeStruct((128, 1024), bf16), jax.ShapeDtypeStruct((128, 256), bf16)
    return pl.pallas_call(
        sum_kernel, in_specs=[VMEM], out_specs=[VMEM] * 4, out_shape=[big, big, small, small],
        compiler_params=pltpu.CompilerParams(vmem_limit_bytes=12 << 20), name="sum_pieces",
    )(pieces)


def make_plan(lengths, core, u, j):
    n = jnp.arange(QT + 1, dtype=i32)[:, None, None]
    x = jnp.arange(4, dtype=i32)[None, :, None]
    t = jnp.arange(16, dtype=i32)[None, None, :]
    pos = (512 * (2 * n + core) + 128 * x + 16 * u + t).reshape(QT + 1, 64)
    docs = jnp.arange(lengths.shape[0])
    ends = jnp.sum(jnp.where(docs[:, None] <= docs[None, :], lengths[:, None], 0), axis=0)
    start = jnp.sum(jnp.where(ends[None, None, :] <= pos[:, :, None], lengths, 0), axis=-1)
    rows = jnp.stack([jnp.tile(pos, (1, 4)), jnp.tile(start, (1, 4))], axis=1).astype(i32)
    low = (start[:QT, 0] // 1024)[None, :]
    plain_low = ((start[:QT, -1] + 1023) // 1024)[None, :]
    d = jnp.arange(KP, dtype=i32)[:, None]
    m = jnp.arange(QT, dtype=i32)[None, :]
    live = (m - d >= 0) & (m - d >= low)
    plain = live & (d > 0) & (m - d >= plain_low)
    code = (m * 256 + m - d).reshape(1, QT * KP)
    order = jnp.arange(QT * KP, dtype=i32)
    earlier = order[:, None] < order[None, :]
    at = jnp.arange(LIST, dtype=i32)[:, None]

    def ranks(mask):
        return jnp.sum((earlier & mask.reshape(QT * KP, 1)).astype(i32), axis=0, keepdims=True)

    def compact(mask, rank):
        mask = mask.reshape(1, QT * KP)
        listed = QT * 256 + jnp.sum(jnp.where(mask & (rank == at), code - QT * 256, 0), axis=1)
        return jnp.where(at[:, 0] == LIST - 1, jnp.sum(mask.astype(i32)), listed)

    rank = ranks(plain)
    plain = plain & (rank.reshape(KP, QT) < jnp.sum(plain.astype(i32)) // TRIP * TRIP)
    edge = live & ~plain
    steps = jnp.stack([compact(plain, rank), compact(edge, ranks(edge))]).astype(i32)
    r = jnp.arange(256, dtype=i32)
    parity = jnp.where(r < 128, core, 1 - core)
    kpos = 512 * parity + 128 * (r % 64 // 16) + 32 * j + 16 * (r // 64 % 2) + r % 16
    return steps, rows, jnp.broadcast_to(kpos[:, None], (256, 128)).astype(i32)


PLANE = ("head", "inner", "zl")


def on_device(query_rows, key_rows, value_rows, out_grad, lengths):
    j, u, core = (lax.axis_index(name) for name in ("head", "inner", "core"))
    swap = [(0, 1), (1, 0)]
    steps, pos, kpos = make_plan(lengths, core, u, j)
    pieces = pack(query_rows.reshape(128, 1024), key_rows.reshape(128, 256), value_rows.reshape(128, 256),
                  out_grad.reshape(128, 1024))
    own = lax.all_to_all(pieces.reshape(64, 16, WIDE), PLANE, 0, 0, tiled=True).reshape(4, QT, 16, WIDE)
    own, steps, pos, kpos = lax.optimization_barrier((own, steps, pos, kpos))
    oth = lax.ppermute(own[..., 512:1024], "core", swap)

    def along(x, k):
        return lax.ppermute(x, "head", [(i, (i + k) % 4) for i in range(4)])

    do = own[..., 1024:]
    dos = [do] + [along(do, k) for k in (1, 2, 3)]
    ot, st = fwd(steps, pos, kpos, own, oth)
    part = delta(st, ot, dos)
    stat, *heads = scale([part] + [along(part, k) for k in (1, 2, 3)], st, ot)
    heads = heads[:1] + [along(heads[k], -k) for k in (1, 2, 3)]
    out, oth_out = bwd(steps, pos, kpos, stat, own, oth, dos, turn_keys(own, oth))
    oth_out, head = gather_parts(oth_out, heads)
    out = add_parts(out, lax.ppermute(oth_out, "core", swap), head)
    out = lax.all_to_all(out.reshape(64, 16, WIDE), PLANE, 0, 0, tiled=True)
    attended, query_grad, key_grad, value_grad = sum_pieces(out)
    return (attended.reshape(1, 1, 128, 1024), query_grad.reshape(1, 1, 128, 1024),
            key_grad.reshape(1, 1, 128, 256), value_grad.reshape(1, 1, 128, 256))


def solution(mesh):
    finer = Mesh(mesh.devices.reshape(4, 8, 2, 2), ("head", "inner", "zl", "core"))
    placed = P(("inner", "zl", "core"), "head", None, None)
    return jax.shard_map(
        on_device,
        mesh=finer,
        in_specs=(placed, placed, placed, placed, P()),
        out_specs=(placed, placed, placed, placed),
        check_vma=False,
    )
```

profile of v0, /device:TPU:0, one launch (start us, length us, event | category | flops | bytes accessed | tf_op | source)
XLA Modules:
  0.0 144.3 jit_solution(10577737693375992813)
XLA Ops:
  0.6 2.7 %pack.1 = bf16[4,16,16,1152]{3,2,1,0:T(8,128)(2,1)} custom-call(bf16[128,1024]{1,0:T(8,128)(2,1)} %bitcast.20, bf16[128,256]{1,0:T(8,128)(2,1)} %bitcast.22, bf16[128,256]{1,0:T(8,128)(2,1)} %bitcast.23, bf16[128,1024]{1,0:T(8,128)(2,1)} %bitcast.21), custom_call_target="tpu_custom_call" | custom-call | tf_op jit(solution)/shard_map/pack/pallas_call | solution.py:314
  3.3 0.0 copy-start
  3.3 11.5 %all-to-all-start = ((bf16[64,16,1152]{2,1,0:T(8,128)(2,1)}), bf16[64,16,1152]{2,1,0:T(8,128)(2,1)S(1)}, u32[]{:S(2)}, u32[]{:S(2)}) async-start(bf16[64,16,1152]{2,1,0:T(8,128)(2,1)} %bitcast.19), calls=%async_computation | async-start | bytes 4718592 | tf_op jit(solution)/shard_map/all_to_all | solution.py:425
  14.9 0.0 copy-done
  14.9 0.1 select_reduce_fusion.3
  15.0 0.1 add.208
  15.1 0.1 add_add_fusion
  15.1 0.1 add.205
  15.2 0.1 add.206
  15.3 0.1 select_reduce_fusion.2
  15.4 0.2 fusion.4
  15.7 0.7 convert_reduce_fusion.2
  17.7 0.1 and.273
  17.7 0.1 and.274
  17.8 0.1 sub.135
  19.2 0.1 ge.113
  19.3 0.1 and.272
  19.4 0.1 tile.18
  19.5 0.1 tile.16
  19.7 0.1 convert_reduce_fusion.1
  19.8 0.6 convert_reduce_fusion.4
  20.4 0.6 convert_reduce_fusion.3
  21.1 0.1 convert_reduce_fusion
  21.2 0.2 select_reduce_fusion.1
  21.4 0.7 compare_select_fusion.1
  22.0 0.7 compare_select_fusion
  22.8 24.5 %all-to-all-done = bf16[64,16,1152]{2,1,0:T(8,128)(2,1)S(1)} async-done(((bf16[64,16,1152]{2,1,0:T(8,128)(2,1)}), bf16[64,16,1152]{2,1,0:T(8,128)(2,1)S(1)}, u32[]{:S(2)}, u32[]{:S(2)}) %all-to-all-start) | async-done | bytes 2359328 | tf_op jit(solution)/shard_map/all_to_all | solution.py:425
  47.2 0.1 broadcast_in_dim.85.kpos_ref
  47.3 0.1 slice.14
  47.5 0.1 collective-permute-start
  47.6 1.2 collective-permute-start.3
  48.8 1.0 collective-permute-start.2
  49.7 0.5 collective-permute-start.1
  50.3 0.0 collective-permute-done.oth_ref
  50.3 13.4 %fwd.1 = (f32[16,128,256]{2,1,0:T(8,128)S(1)}, f32[16,4,256]{2,1,0:T(4,128)S(1)}) custom-call(s32[2,160]{1,0:T(2,128)S(1)} %pad_add_fusion.1.steps, s32[17,2,256]{2,1,0:T(2,128)S(1)} %pad_add_fusion.pos_ref, s32[256,128]{1,0:T(8,128)S(1)} %broadcast_in_dim.85.kpos_ref, bf16[4,16,16,1152]{3,2,1,0:T(8,128)(2,1)S(1)} %bitcast.15, ...), custom_call_target="tpu_custom_call" | custom-call | flops 15000000512 | bytes 8388608 | tf_op jit(solution)/shard_map/fwd/pallas_call | solution.py:223
  63.7 0.0 collective-permute-done.3.do3_ref
  63.7 0.0 collective-permute-done.2.do2_ref
  63.7 0.6 collective-permute-done.1.do1_ref
  64.3 0.6 delta.1.st0_ref
  64.9 2.2 %collective-permute-start.6 = (f32[16,2,256]{2,1,0:T(2,128)S(1)}, f32[16,2,256]{2,1,0:T(2,128)S(1)}, u32[]{:S(2)}, u32[]{:S(2)}) collective-permute-start(f32[16,2,256]{2,1,0:T(2,128)S(1)} %delta.1.st0_ref), channel_id=1, source_target_pairs={{0,96},{32,0},{64,32},{96,64},{1,97},{33,1},{65,33},{97,65},{2,98}... | collective-permute-start | bytes 98312 | tf_op jit(solution)/shard_map/ppermute | solution.py:430
  67.0 1.4 collective-permute-start.5
  68.4 0.9 collective-permute-start.4
  69.3 0.5 turn_keys.1.kt
  69.8 0.0 collective-permute-done.6.st3_ref
  69.8 2.6 %collective-permute-done.5.st2_ref = f32[16,2,256]{2,1,0:T(2,128)S(1)} collective-permute-done((f32[16,2,256]{2,1,0:T(2,128)S(1)}, f32[16,2,256]{2,1,0:T(2,128)S(1)}, u32[]{:S(2)}, u32[]{:S(2)}) %collective-permute-start.5) | collective-permute-done | bytes 32800 | tf_op jit(solution)/shard_map/ppermute | solution.py:430
  72.5 1.1 collective-permute-done.4.st1_ref
  73.5 1.0 scale.1
  74.5 0.4 collective-permute-start.7
  75.0 1.4 collective-permute-start.8
  76.4 0.6 collective-permute-start.9
  77.0 21.9 %bwd.1 = (bf16[4,16,16,1152]{3,2,1,0:T(8,128)(2,1)S(1)}, bf16[4,16,16,512]{3,2,1,0:T(8,128)(2,1)S(1)}) custom-call(s32[2,160]{1,0:T(2,128)S(1)} %pad_add_fusion.1.steps, s32[17,2,256]{2,1,0:T(2,128)S(1)} %pad_add_fusion.pos_ref, s32[256,128]{1,0:T(8,128)S(1)} %broadcast_in_dim.85.kpos_ref, f32[17,2,256]{2,1,0:T(2,128)S(1)} %get-tuple-element.29.stat_ref, ...), custom_call_target="tpu_custom_call" | custom-call | flops 24999999488 | bytes 8388608 | tf_op jit(solution)/shard_map/bwd/pallas_call | solution.py:269
  98.9 0.0 collective-permute-done.7.o1_ref
  98.9 0.0 collective-permute-done.8.o2_ref
  98.9 0.0 collective-permute-done.9.o3_ref
  98.9 0.2 gather_parts.1
  99.1 0.1 collective-permute-start.10
  99.2 2.6 %collective-permute-done.10.other_ref = bf16[4,16,16,512]{3,2,1,0:T(8,128)(2,1)S(1)} collective-permute-done((bf16[4,16,16,512]{3,2,1,0:T(8,128)(2,1)S(1)}, bf16[4,16,16,512]{3,2,1,0:T(8,128)(2,1)S(1)}, u32[]{:S(2)}, u32[]{:S(2)}) %collective-permute-start.10) | collective-permute-done | bytes 1048608 | tf_op jit(solution)/shard_map/ppermute | solution.py:440
  101.9 0.5 add_parts.1
  102.4 40.9 %all_to_all.10.in_ref = bf16[64,16,1152]{2,1,0:T(8,128)(2,1)S(1)} all-to-all(bf16[64,16,1152]{2,1,0:T(8,128)(2,1)S(1)} %bitcast.18), channel_id=1, replica_groups=mesh['head'=4,'inner'=8,'zl'=2,'core'=2] {'head','inner','zl'}, dimensions={0} | all-to-all | bytes 4718592 | tf_op jit(solution)/shard_map/all_to_all | solution.py:441
  143.4 1.0 sum_pieces.1
  (19 shorter events, 0.2 us)
Async XLA Ops:
  3.3 11.6 %copy-start = (s32[4]{0:T(128)S(1)}, s32[4]{0:T(128)}, u32[]{:S(2)}) copy-start(s32[4]{0:T(128)} %param.9) | copy-start | bytes 52
  3.3 43.9 %all-to-all-start = ((bf16[64,16,1152]{2,1,0:T(8,128)(2,1)}), bf16[64,16,1152]{2,1,0:T(8,128)(2,1)S(1)}, u32[]{:S(2)}, u32[]{:S(2)}) async-start(bf16[64,16,1152]{2,1,0:T(8,128)(2,1)} %bitcast.19), calls=%async_computation | async-start | bytes 4718592 | tf_op jit(solution)/shard_map/all_to_all | solution.py:425
  47.5 2.8 %collective-permute-start = (bf16[4,16,16,512]{3,2,1,0:T(8,128)(2,1)S(1)}, bf16[4,16,16,512]{3,2,1,0:T(8,128)(2,1)S(1)}, u32[]{:S(2)}, u32[]{:S(2)}) collective-permute-start(bf16[4,16,16,512]{3,2,1,0:T(8,128)(2,1)S(1)} %slice.14), channel_id=1, source_target_pairs={{0,1},{1,0},{2,3},{3,2},{4,5},{5,4},{6,7},{7,6},{8,9},{9,8},{10,11... | collective-permute-start | bytes 3145736 | tf_op jit(solution)/shard_map/ppermute | solution.py:427
  47.6 16.1 %collective-permute-start.3 = (bf16[4,16,16,128]{3,2,1,0:T(8,128)(2,1)S(1)}, bf16[4,16,16,128]{3,2,1,0:T(8,128)(2,1)S(1)}, u32[]{:S(2)}, u32[]{:S(2)}) collective-permute-start(bf16[4,16,16,128]{3,2,1,0:T(8,128)(2,1)S(1)} %slice.15.do0_ref), channel_id=1, source_target_pairs={{0,96},{32,0},{64,32},{96,64},{1,97},{33,1},{65,33},{97,65},{2,98}... | collective-permute-start | bytes 786440 | tf_op jit(solution)/shard_map/ppermute | solution.py:430
  48.8 14.9 %collective-permute-start.2 = (bf16[4,16,16,128]{3,2,1,0:T(8,128)(2,1)S(1)}, bf16[4,16,16,128]{3,2,1,0:T(8,128)(2,1)S(1)}, u32[]{:S(2)}, u32[]{:S(2)}) collective-permute-start(bf16[4,16,16,128]{3,2,1,0:T(8,128)(2,1)S(1)} %slice.15.do0_ref), channel_id=1, source_target_pairs={{0,64},{32,96},{64,0},{96,32},{1,65},{33,97},{65,1},{97,33},{2,66}... | collective-permute-start | bytes 786440 | tf_op jit(solution)/shard_map/ppermute | solution.py:430
  49.7 14.6 %collective-permute-start.1 = (bf16[4,16,16,128]{3,2,1,0:T(8,128)(2,1)S(1)}, bf16[4,16,16,128]{3,2,1,0:T(8,128)(2,1)S(1)}, u32[]{:S(2)}, u32[]{:S(2)}) collective-permute-start(bf16[4,16,16,128]{3,2,1,0:T(8,128)(2,1)S(1)} %slice.15.do0_ref), channel_id=1, source_target_pairs={{0,32},{32,64},{64,96},{96,0},{1,33},{33,65},{65,97},{97,1},{2,34}... | collective-permute-start | bytes 786440 | tf_op jit(solution)/shard_map/ppermute | solution.py:430
  64.9 4.9 %collective-permute-start.6 = (f32[16,2,256]{2,1,0:T(2,128)S(1)}, f32[16,2,256]{2,1,0:T(2,128)S(1)}, u32[]{:S(2)}, u32[]{:S(2)}) collective-permute-start(f32[16,2,256]{2,1,0:T(2,128)S(1)} %delta.1.st0_ref), channel_id=1, source_target_pairs={{0,96},{32,0},{64,32},{96,64},{1,97},{33,1},{65,33},{97,65},{2,98}... | collective-permute-start | bytes 98312 | tf_op jit(solution)/shard_map/ppermute | solution.py:430
  67.0 5.4 %collective-permute-start.5 = (f32[16,2,256]{2,1,0:T(2,128)S(1)}, f32[16,2,256]{2,1,0:T(2,128)S(1)}, u32[]{:S(2)}, u32[]{:S(2)}) collective-permute-start(f32[16,2,256]{2,1,0:T(2,128)S(1)} %delta.1.st0_ref), channel_id=1, source_target_pairs={{0,64},{32,96},{64,0},{96,32},{1,65},{33,97},{65,1},{97,33},{2,66}... | collective-permute-start | bytes 98312 | tf_op jit(solution)/shard_map/ppermute | solution.py:430
  68.4 5.1 %collective-permute-start.4 = (f32[16,2,256]{2,1,0:T(2,128)S(1)}, f32[16,2,256]{2,1,0:T(2,128)S(1)}, u32[]{:S(2)}, u32[]{:S(2)}) collective-permute-start(f32[16,2,256]{2,1,0:T(2,128)S(1)} %delta.1.st0_ref), channel_id=1, source_target_pairs={{0,32},{32,64},{64,96},{96,0},{1,33},{33,65},{65,97},{97,1},{2,34}... | collective-permute-start | bytes 98312 | tf_op jit(solution)/shard_map/ppermute | solution.py:430
  74.5 24.4 %collective-permute-start.7 = (bf16[4,16,16,128]{3,2,1,0:T(8,128)(2,1)S(1)}, bf16[4,16,16,128]{3,2,1,0:T(8,128)(2,1)S(1)}, u32[]{:S(2)}, u32[]{:S(2)}) collective-permute-start(bf16[4,16,16,128]{3,2,1,0:T(8,128)(2,1)S(1)} %get-tuple-element.33), channel_id=1, source_target_pairs={{0,96},{32,0},{64,32},{96,64},{1,97},{33,1},{65,33},{97,65},{2,98}... | collective-permute-start | bytes 786440 | tf_op jit(solution)/shard_map/ppermute | solution.py:430
  75.0 24.0 %collective-permute-start.8 = (bf16[4,16,16,128]{3,2,1,0:T(8,128)(2,1)S(1)}, bf16[4,16,16,128]{3,2,1,0:T(8,128)(2,1)S(1)}, u32[]{:S(2)}, u32[]{:S(2)}) collective-permute-start(bf16[4,16,16,128]{3,2,1,0:T(8,128)(2,1)S(1)} %get-tuple-element.34), channel_id=1, source_target_pairs={{0,64},{32,96},{64,0},{96,32},{1,65},{33,97},{65,1},{97,33},{2,66}... | collective-permute-start | bytes 786440 | tf_op jit(solution)/shard_map/ppermute | solution.py:430
  76.4 22.6 %collective-permute-start.9 = (bf16[4,16,16,128]{3,2,1,0:T(8,128)(2,1)S(1)}, bf16[4,16,16,128]{3,2,1,0:T(8,128)(2,1)S(1)}, u32[]{:S(2)}, u32[]{:S(2)}) collective-permute-start(bf16[4,16,16,128]{3,2,1,0:T(8,128)(2,1)S(1)} %get-tuple-element.35), channel_id=1, source_target_pairs={{0,32},{32,64},{64,96},{96,0},{1,33},{33,65},{65,97},{97,1},{2,34}... | collective-permute-start | bytes 786440 | tf_op jit(solution)/shard_map/ppermute | solution.py:430
  99.1 2.7 %collective-permute-start.10 = (bf16[4,16,16,512]{3,2,1,0:T(8,128)(2,1)S(1)}, bf16[4,16,16,512]{3,2,1,0:T(8,128)(2,1)S(1)}, u32[]{:S(2)}, u32[]{:S(2)}) collective-permute-start(bf16[4,16,16,512]{3,2,1,0:T(8,128)(2,1)S(1)} %get-tuple-element.36), channel_id=1, source_target_pairs={{0,1},{1,0},{2,3},{3,2},{4,5},{5,4},{6,7},{7,6},{8,9},{9,8},{10,11... | collective-permute-start | bytes 3145736 | tf_op jit(solution)/shard_map/ppermute | solution.py:440
where the time goes:
time: 142 us; the launch traced here: 144 us
  Pallas kernels  41.7 us (29%)
  blocking collectives  40.9 us (29%)
  waiting for transfers between devices  31.5 us (22%)
  starting transfers between devices  21.2 us (15%)
  other arithmetic  4.24 us (3%)
  between operations  3.61 us (3%)
    all_to_all x1, blocking collectives, on_device(): out = lax.all_to_all(out.reshape(64, 16, WIDE), PLANE, 0, 0, tiled=True)  40.9 us
    all_to_all x1, waiting for transfers between devices, on_device(): lax.all_to_all(pieces.reshape(64, 16, WIDE), PLANE, 0, 0, tiled=True)  24.5 us
    pallas_call x1, Pallas kernels, bwd(): pl.pallas_call(bwd_kernel, in_specs=[SMEM] + [VMEM] * 10, out_specs=[VMEM...  21.9 us
    pallas_call x1, Pallas kernels, fwd(): pl.pallas_call(fwd_kernel, in_specs=[SMEM] + [VMEM] * 4, out_specs=[VMEM,...  13.4 us
    all_to_all x1, starting transfers between devices, on_device(): lax.all_to_all(pieces.reshape(64, 16, WIDE), PLANE, 0, 0, tiled=True)  11.5 us
    ppermute x9, starting transfers between devices, along(): return lax.ppermute(x, 'head', [(i, (i + k) % 4) for i in range(4)])  9.56 us
    ppermute x9, waiting for transfers between devices, along(): return lax.ppermute(x, 'head', [(i, (i + k) % 4) for i in range(4)])  4.34 us
  transfers between devices with their start and end apart: 12, of which 5 were waited for; matrix products, arithmetic and copies ran while one was open for 4% of the time, Pallas kernels for 25%

commit v1 on v0

--- a/solution.py
+++ b/solution.py
@@ -95,7 +95,7 @@
                 soften(t + half + 4 + k, nxt + k)
 
 
-def fwd_kernel(steps, pos_ref, kpos_ref, own_ref, oth_ref, ot_ref, st_ref, vt, m_s, l_s, acc, s_buf, p_buf, a_buf):
+def fwd_kernel(steps, pos_ref, kpos_ref, own_ref, oth_ref, acc, st_ref, vt, m_s, l_s, s_buf, p_buf, a_buf):
     @pl.loop(0, KP, unroll=4)
     def _(p):
         vt[:, pl.ds(pl.multiple_of(p * 256, 256), 256)] = key_tile(own_ref, oth_ref, p, HD).T
@@ -136,8 +136,6 @@
 
     @pl.loop(0, QT, unroll=4)
     def _(n):
-        o = acc[n]
-        ot_ref[n] = o
         st_ref[n, 0:1, :] = m_s[n]
         st_ref[n, 1:2, :] = l_s[n]
 
@@ -226,10 +224,10 @@
         out_specs=[VMEM, VMEM],
         scratch_shapes=[
             pltpu.VMEM((HD, KP * 256), bf16),
-            pltpu.VMEM((QT + 1, 1, 256), f32), pltpu.VMEM((QT + 1, 1, 256), f32), pltpu.VMEM((QT + 1, HD, 256), f32),
+            pltpu.VMEM((QT + 1, 1, 256), f32), pltpu.VMEM((QT + 1, 1, 256), f32),
             pltpu.VMEM((4, 256, 256), f32), pltpu.VMEM((4, 256, 256), bf16), pltpu.VMEM((4, 1, 256), f32),
         ],
-        out_shape=[jax.ShapeDtypeStruct((QT, HD, 256), f32), jax.ShapeDtypeStruct((QT, 4, 256), f32)],
+        out_shape=[jax.ShapeDtypeStruct((QT + 1, HD, 256), f32), jax.ShapeDtypeStruct((QT, 4, 256), f32)],
         compiler_params=pltpu.CompilerParams(vmem_limit_bytes=16 << 20),
         cost_estimate=pl.CostEstimate(flops=15 * 10 ** 9, bytes_accessed=8 << 20, transcendentals=0),
         name="fwd",
@@ -429,12 +427,16 @@
     def along(x, k):
         return lax.ppermute(x, "head", [(i, (i + k) % 4) for i in range(4)])
 
+    def spread(arrays, sign):
+        moved = {k: along(arrays[k], sign * k) for k in (3, 1, 2)}
+        return [arrays[0]] + [moved[k] for k in (1, 2, 3)]
+
     do = own[..., 1024:]
-    dos = [do] + [along(do, k) for k in (1, 2, 3)]
+    dos = spread([do] * 4, 1)
     ot, st = fwd(steps, pos, kpos, own, oth)
     part = delta(st, ot, dos)
-    stat, *heads = scale([part] + [along(part, k) for k in (1, 2, 3)], st, ot)
-    heads = heads[:1] + [along(heads[k], -k) for k in (1, 2, 3)]
+    stat, *heads = scale(spread([part] * 4, 1), st, ot)
+    heads = spread(heads, -1)
     out, oth_out = bwd(steps, pos, kpos, stat, own, oth, dos, turn_keys(own, oth))
     oth_out, head = gather_parts(oth_out, heads)
     out = add_parts(out, lax.ppermute(oth_out, "core", swap), head)

time: 142 us -> 142 us (level); the launches traced: 144 us -> 140 us
  Pallas kernels: 41.7 us -> 36.8 us
  waiting for transfers between devices: 31.5 us -> 33.4 us
    pallas_call x1, Pallas kernels: 21.9 us -> 18.9 us  [bwd(): pl.pallas_call(bwd_kernel, in_specs=[SMEM] + [VMEM] * 10, out_specs=[VMEM...]
    ppermute x9, waiting for transfers between devices: 4.34 us -> 6.27 us  [along(): return lax.ppermute(x, 'head', [(i, (i + k) % 4) for i in range(4)])]
    pallas_call x1, Pallas kernels: 13.4 us -> 11.5 us  [fwd(): pl.pallas_call(fwd_kernel, in_specs=[SMEM] + [VMEM] * 4, out_specs=[VMEM,...]
  transfers between devices with their start and end apart: 12 -> 12, of which waited for: 5 -> 6; matrix products, arithmetic and copies ran while one was open for 4% -> 4% of each run, Pallas kernels for 25% -> 22%
where the time goes in v1:
time: 142 us; the launch traced here: 140 us
  blocking collectives  40.6 us (29%)
  Pallas kernels  36.8 us (26%)
  waiting for transfers between devices  33.4 us (24%)
  starting transfers between devices  19.8 us (14%)
  other arithmetic  4.24 us (3%)
  between operations  3.6 us (3%)
    all_to_all x1, blocking collectives, on_device(): out = lax.all_to_all(out.reshape(64, 16, WIDE), PLANE, 0, 0, tiled=True)  40.6 us
    all_to_all x1, waiting for transfers between devices, on_device(): lax.all_to_all(pieces.reshape(64, 16, WIDE), PLANE, 0, 0, tiled=True)  24.5 us
    pallas_call x1, Pallas kernels, bwd(): pl.pallas_call(bwd_kernel, in_specs=[SMEM] + [VMEM] * 10, out_specs=[VMEM...  18.9 us
    all_to_all x1, starting transfers between devices, on_device(): lax.all_to_all(pieces.reshape(64, 16, WIDE), PLANE, 0, 0, tiled=True)  11.5 us
    pallas_call x1, Pallas kernels, fwd(): pl.pallas_call(fwd_kernel, in_specs=[SMEM] + [VMEM] * 4, out_specs=[VMEM,...  11.5 us
    ppermute x9, starting transfers between devices, along(): return lax.ppermute(x, 'head', [(i, (i + k) % 4) for i in range(4)])  8.14 us
    ppermute x9, waiting for transfers between devices, along(): return lax.ppermute(x, 'head', [(i, (i + k) % 4) for i in range(4)])  6.27 us
  transfers between devices with their start and end apart: 12, of which 6 were waited for; matrix products, arithmetic and copies ran while one was open for 4% of the time, Pallas kernels for 22%

profile of v1, /device:TPU:0, one launch (start us, length us, event | category | flops | bytes accessed | tf_op | source)
XLA Modules:
  0.0 139.5 jit_solution(15774846657546656950)
XLA Ops:
  0.6 2.7 %pack.1 = bf16[4,16,16,1152]{3,2,1,0:T(8,128)(2,1)} custom-call(bf16[128,1024]{1,0:T(8,128)(2,1)} %bitcast.20, bf16[128,256]{1,0:T(8,128)(2,1)} %bitcast.22, bf16[128,256]{1,0:T(8,128)(2,1)} %bitcast.23, bf16[128,1024]{1,0:T(8,128)(2,1)} %bitcast.21), custom_call_target="tpu_custom_call" | custom-call | tf_op jit(solution)/shard_map/pack/pallas_call | solution.py:312
  3.3 0.0 copy-start
  3.3 11.5 %all-to-all-start = ((bf16[64,16,1152]{2,1,0:T(8,128)(2,1)}), bf16[64,16,1152]{2,1,0:T(8,128)(2,1)S(1)}, u32[]{:S(2)}, u32[]{:S(2)}) async-start(bf16[64,16,1152]{2,1,0:T(8,128)(2,1)} %bitcast.19), calls=%async_computation | async-start | bytes 4718592 | tf_op jit(solution)/shard_map/all_to_all | solution.py:423
  14.9 0.0 copy-done
  14.9 0.1 select_reduce_fusion.3
  15.0 0.1 add.208
  15.1 0.1 add_add_fusion
  15.1 0.1 add.205
  15.2 0.1 add.206
  15.3 0.1 select_reduce_fusion.2
  15.4 0.2 fusion.4
  15.7 0.7 convert_reduce_fusion.2
  17.7 0.1 and.273
  17.7 0.1 and.274
  17.8 0.1 sub.135
  19.2 0.1 ge.113
  19.3 0.1 and.272
  19.4 0.1 tile.18
  19.5 0.1 tile.16
  19.7 0.1 convert_reduce_fusion.1
  19.8 0.6 convert_reduce_fusion.4
  20.4 0.6 convert_reduce_fusion.3
  21.1 0.1 convert_reduce_fusion
  21.2 0.2 select_reduce_fusion.1
  21.4 0.7 compare_select_fusion.1
  22.0 0.7 compare_select_fusion
  22.8 24.5 %all-to-all-done = bf16[64,16,1152]{2,1,0:T(8,128)(2,1)S(1)} async-done(((bf16[64,16,1152]{2,1,0:T(8,128)(2,1)}), bf16[64,16,1152]{2,1,0:T(8,128)(2,1)S(1)}, u32[]{:S(2)}, u32[]{:S(2)}) %all-to-all-start) | async-done | bytes 2359328 | tf_op jit(solution)/shard_map/all_to_all | solution.py:423
  47.2 0.1 broadcast_in_dim.85.kpos_ref
  47.3 0.1 slice.14
  47.5 0.1 collective-permute-start
  47.6 1.2 collective-permute-start.3
  48.8 1.0 collective-permute-start.2
  49.7 0.5 collective-permute-start.1
  50.3 0.0 collective-permute-done.oth_ref
  50.3 11.5 %fwd.1 = (f32[17,128,256]{2,1,0:T(8,128)S(1)}, f32[16,4,256]{2,1,0:T(4,128)S(1)}) custom-call(s32[2,160]{1,0:T(2,128)S(1)} %pad_add_fusion.1.steps, s32[17,2,256]{2,1,0:T(2,128)S(1)} %pad_add_fusion.pos_ref, s32[256,128]{1,0:T(8,128)S(1)} %broadcast_in_dim.85.kpos_ref, bf16[4,16,16,1152]{3,2,1,0:T(8,128)(2,1)S(1)} %bitcast.15, ...), custom_call_target="tpu_custom_call" | custom-call | flops 15000000512 | bytes 8388608 | tf_op jit(solution)/shard_map/fwd/pallas_call | solution.py:221
  61.8 0.0 collective-permute-done.3.do3_ref
  61.8 0.0 collective-permute-done.2.do2_ref
  61.8 2.5 %collective-permute-done.1.do1_ref = bf16[4,16,16,128]{3,2,1,0:T(8,128)(2,1)S(1)} collective-permute-done((bf16[4,16,16,128]{3,2,1,0:T(8,128)(2,1)S(1)}, bf16[4,16,16,128]{3,2,1,0:T(8,128)(2,1)S(1)}, u32[]{:S(2)}, u32[]{:S(2)}) %collective-permute-start.1) | collective-permute-done | bytes 262176 | tf_op jit(solution)/shard_map/ppermute | solution.py:428
  64.3 0.6 delta.1.st0_ref
  64.9 0.7 collective-permute-start.6
  65.6 1.0 collective-permute-start.5
  66.5 0.9 collective-permute-start.4
  67.4 0.5 turn_keys.1.kt
  67.9 1.0 collective-permute-done.6.st3_ref
  68.9 2.1 %collective-permute-done.5.st2_ref = f32[16,2,256]{2,1,0:T(2,128)S(1)} collective-permute-done((f32[16,2,256]{2,1,0:T(2,128)S(1)}, f32[16,2,256]{2,1,0:T(2,128)S(1)}, u32[]{:S(2)}, u32[]{:S(2)}) %collective-permute-start.5) | collective-permute-done | bytes 32800 | tf_op jit(solution)/shard_map/ppermute | solution.py:428
  71.0 0.7 collective-permute-done.4.st1_ref
  71.7 1.0 scale.1
  72.7 2.0 %collective-permute-start.7 = (bf16[4,16,16,128]{3,2,1,0:T(8,128)(2,1)S(1)}, bf16[4,16,16,128]{3,2,1,0:T(8,128)(2,1)S(1)}, u32[]{:S(2)}, u32[]{:S(2)}) collective-permute-start(bf16[4,16,16,128]{3,2,1,0:T(8,128)(2,1)S(1)} %get-tuple-element.33), channel_id=1, source_target_pairs={{0,96},{32,0},{64,32},{96,64},{1,97},{33,1},{65,33},{97,65},{2,98}... | collective-permute-start | bytes 786440 | tf_op jit(solution)/shard_map/ppermute | solution.py:428
  74.6 0.9 collective-permute-start.8
  75.5 0.0 collective-permute-start.9
  75.6 18.9 %bwd.1 = (bf16[4,16,16,1152]{3,2,1,0:T(8,128)(2,1)S(1)}, bf16[4,16,16,512]{3,2,1,0:T(8,128)(2,1)S(1)}) custom-call(s32[2,160]{1,0:T(2,128)S(1)} %pad_add_fusion.1.steps, s32[17,2,256]{2,1,0:T(2,128)S(1)} %pad_add_fusion.pos_ref, s32[256,128]{1,0:T(8,128)S(1)} %broadcast_in_dim.85.kpos_ref, f32[17,2,256]{2,1,0:T(2,128)S(1)} %get-tuple-element.29.stat_ref, ...), custom_call_target="tpu_custom_call" | custom-call | flops 24999999488 | bytes 8388608 | tf_op jit(solution)/shard_map/bwd/pallas_call | solution.py:267
  94.5 0.0 collective-permute-done.7.o1_ref
  94.5 0.0 collective-permute-done.8.o2_ref
  94.5 0.0 collective-permute-done.9.o3_ref
  94.5 0.2 gather_parts.1
  94.7 0.1 collective-permute-start.10
  94.8 2.6 %collective-permute-done.10.other_ref = bf16[4,16,16,512]{3,2,1,0:T(8,128)(2,1)S(1)} collective-permute-done((bf16[4,16,16,512]{3,2,1,0:T(8,128)(2,1)S(1)}, bf16[4,16,16,512]{3,2,1,0:T(8,128)(2,1)S(1)}, u32[]{:S(2)}, u32[]{:S(2)}) %collective-permute-start.10) | collective-permute-done | bytes 1048608 | tf_op jit(solution)/shard_map/ppermute | solution.py:442
  97.5 0.5 add_parts.1
  98.0 40.6 %all_to_all.10.in_ref = bf16[64,16,1152]{2,1,0:T(8,128)(2,1)S(1)} all-to-all(bf16[64,16,1152]{2,1,0:T(8,128)(2,1)S(1)} %bitcast.18), channel_id=1, replica_groups=mesh['head'=4,'inner'=8,'zl'=2,'core'=2] {'head','inner','zl'}, dimensions={0} | all-to-all | bytes 4718592 | tf_op jit(solution)/shard_map/all_to_all | solution.py:443
  138.6 1.0 sum_pieces.1
  (19 shorter events, 0.2 us)
Async XLA Ops:
  3.3 11.6 %copy-start = (s32[4]{0:T(128)S(1)}, s32[4]{0:T(128)}, u32[]{:S(2)}) copy-start(s32[4]{0:T(128)} %param.9) | copy-start | bytes 52
  3.3 43.9 %all-to-all-start = ((bf16[64,16,1152]{2,1,0:T(8,128)(2,1)}), bf16[64,16,1152]{2,1,0:T(8,128)(2,1)S(1)}, u32[]{:S(2)}, u32[]{:S(2)}) async-start(bf16[64,16,1152]{2,1,0:T(8,128)(2,1)} %bitcast.19), calls=%async_computation | async-start | bytes 4718592 | tf_op jit(solution)/shard_map/all_to_all | solution.py:423
  47.5 2.8 %collective-permute-start = (bf16[4,16,16,512]{3,2,1,0:T(8,128)(2,1)S(1)}, bf16[4,16,16,512]{3,2,1,0:T(8,128)(2,1)S(1)}, u32[]{:S(2)}, u32[]{:S(2)}) collective-permute-start(bf16[4,16,16,512]{3,2,1,0:T(8,128)(2,1)S(1)} %slice.14), channel_id=1, source_target_pairs={{0,1},{1,0},{2,3},{3,2},{4,5},{5,4},{6,7},{7,6},{8,9},{9,8},{10,11... | collective-permute-start | bytes 3145736 | tf_op jit(solution)/shard_map/ppermute | solution.py:425
  47.6 14.2 %collective-permute-start.3 = (bf16[4,16,16,128]{3,2,1,0:T(8,128)(2,1)S(1)}, bf16[4,16,16,128]{3,2,1,0:T(8,128)(2,1)S(1)}, u32[]{:S(2)}, u32[]{:S(2)}) collective-permute-start(bf16[4,16,16,128]{3,2,1,0:T(8,128)(2,1)S(1)} %slice.15.do0_ref), channel_id=1, source_target_pairs={{0,96},{32,0},{64,32},{96,64},{1,97},{33,1},{65,33},{97,65},{2,98}... | collective-permute-start | bytes 786440 | tf_op jit(solution)/shard_map/ppermute | solution.py:428
  48.8 13.0 %collective-permute-start.2 = (bf16[4,16,16,128]{3,2,1,0:T(8,128)(2,1)S(1)}, bf16[4,16,16,128]{3,2,1,0:T(8,128)(2,1)S(1)}, u32[]{:S(2)}, u32[]{:S(2)}) collective-permute-start(bf16[4,16,16,128]{3,2,1,0:T(8,128)(2,1)S(1)} %slice.15.do0_ref), channel_id=1, source_target_pairs={{0,64},{32,96},{64,0},{96,32},{1,65},{33,97},{65,1},{97,33},{2,66}... | collective-permute-start | bytes 786440 | tf_op jit(solution)/shard_map/ppermute | solution.py:428
  49.7 14.6 %collective-permute-start.1 = (bf16[4,16,16,128]{3,2,1,0:T(8,128)(2,1)S(1)}, bf16[4,16,16,128]{3,2,1,0:T(8,128)(2,1)S(1)}, u32[]{:S(2)}, u32[]{:S(2)}) collective-permute-start(bf16[4,16,16,128]{3,2,1,0:T(8,128)(2,1)S(1)} %slice.15.do0_ref), channel_id=1, source_target_pairs={{0,32},{32,64},{64,96},{96,0},{1,33},{33,65},{65,97},{97,1},{2,34}... | collective-permute-start | bytes 786440 | tf_op jit(solution)/shard_map/ppermute | solution.py:428
  64.9 4.0 %collective-permute-start.6 = (f32[16,2,256]{2,1,0:T(2,128)S(1)}, f32[16,2,256]{2,1,0:T(2,128)S(1)}, u32[]{:S(2)}, u32[]{:S(2)}) collective-permute-start(f32[16,2,256]{2,1,0:T(2,128)S(1)} %delta.1.st0_ref), channel_id=1, source_target_pairs={{0,96},{32,0},{64,32},{96,64},{1,97},{33,1},{65,33},{97,65},{2,98}... | collective-permute-start | bytes 98312 | tf_op jit(solution)/shard_map/ppermute | solution.py:428
  65.6 5.4 %collective-permute-start.5 = (f32[16,2,256]{2,1,0:T(2,128)S(1)}, f32[16,2,256]{2,1,0:T(2,128)S(1)}, u32[]{:S(2)}, u32[]{:S(2)}) collective-permute-start(f32[16,2,256]{2,1,0:T(2,128)S(1)} %delta.1.st0_ref), channel_id=1, source_target_pairs={{0,64},{32,96},{64,0},{96,32},{1,65},{33,97},{65,1},{97,33},{2,66}... | collective-permute-start | bytes 98312 | tf_op jit(solution)/shard_map/ppermute | solution.py:428
  66.5 5.1 %collective-permute-start.4 = (f32[16,2,256]{2,1,0:T(2,128)S(1)}, f32[16,2,256]{2,1,0:T(2,128)S(1)}, u32[]{:S(2)}, u32[]{:S(2)}) collective-permute-start(f32[16,2,256]{2,1,0:T(2,128)S(1)} %delta.1.st0_ref), channel_id=1, source_target_pairs={{0,32},{32,64},{64,96},{96,0},{1,33},{33,65},{65,97},{97,1},{2,34}... | collective-permute-start | bytes 98312 | tf_op jit(solution)/shard_map/ppermute | solution.py:428
  72.7 21.8 %collective-permute-start.7 = (bf16[4,16,16,128]{3,2,1,0:T(8,128)(2,1)S(1)}, bf16[4,16,16,128]{3,2,1,0:T(8,128)(2,1)S(1)}, u32[]{:S(2)}, u32[]{:S(2)}) collective-permute-start(bf16[4,16,16,128]{3,2,1,0:T(8,128)(2,1)S(1)} %get-tuple-element.33), channel_id=1, source_target_pairs={{0,96},{32,0},{64,32},{96,64},{1,97},{33,1},{65,33},{97,65},{2,98}... | collective-permute-start | bytes 786440 | tf_op jit(solution)/shard_map/ppermute | solution.py:428
  74.6 19.9 %collective-permute-start.8 = (bf16[4,16,16,128]{3,2,1,0:T(8,128)(2,1)S(1)}, bf16[4,16,16,128]{3,2,1,0:T(8,128)(2,1)S(1)}, u32[]{:S(2)}, u32[]{:S(2)}) collective-permute-start(bf16[4,16,16,128]{3,2,1,0:T(8,128)(2,1)S(1)} %get-tuple-element.34), channel_id=1, source_target_pairs={{0,64},{32,96},{64,0},{96,32},{1,65},{33,97},{65,1},{97,33},{2,66}... | collective-permute-start | bytes 786440 | tf_op jit(solution)/shard_map/ppermute | solution.py:428
  75.5 19.0 %collective-permute-start.9 = (bf16[4,16,16,128]{3,2,1,0:T(8,128)(2,1)S(1)}, bf16[4,16,16,128]{3,2,1,0:T(8,128)(2,1)S(1)}, u32[]{:S(2)}, u32[]{:S(2)}) collective-permute-start(bf16[4,16,16,128]{3,2,1,0:T(8,128)(2,1)S(1)} %get-tuple-element.35), channel_id=1, source_target_pairs={{0,32},{32,64},{64,96},{96,0},{1,33},{33,65},{65,97},{97,1},{2,34}... | collective-permute-start | bytes 786440 | tf_op jit(solution)/shard_map/ppermute | solution.py:428
  94.7 2.7 %collective-permute-start.10 = (bf16[4,16,16,512]{3,2,1,0:T(8,128)(2,1)S(1)}, bf16[4,16,16,512]{3,2,1,0:T(8,128)(2,1)S(1)}, u32[]{:S(2)}, u32[]{:S(2)}) collective-permute-start(bf16[4,16,16,512]{3,2,1,0:T(8,128)(2,1)S(1)} %get-tuple-element.36), channel_id=1, source_target_pairs={{0,1},{1,0},{2,3},{3,2},{4,5},{5,4},{6,7},{7,6},{8,9},{9,8},{10,11... | collective-permute-start | bytes 3145736 | tf_op jit(solution)/shard_map/ppermute | solution.py:442

commit v2 on v1

--- a/solution.py
+++ b/solution.py
@@ -96,7 +96,7 @@
 
 
 def fwd_kernel(steps, pos_ref, kpos_ref, own_ref, oth_ref, acc, st_ref, vt, m_s, l_s, s_buf, p_buf, a_buf):
-    @pl.loop(0, KP, unroll=4)
+    @pl.loop(0, KP, unroll=8)
     def _(p):
         vt[:, pl.ds(pl.multiple_of(p * 256, 256), 256)] = key_tile(own_ref, oth_ref, p, HD).T
 
@@ -134,7 +134,7 @@
     run(0)
     run(1)
 
-    @pl.loop(0, QT, unroll=4)
+    @pl.loop(0, QT, unroll=8)
     def _(n):
         st_ref[n, 0:1, :] = m_s[n]
         st_ref[n, 1:2, :] = l_s[n]
@@ -143,7 +143,7 @@
 def delta_kernel(st_ref, ot_ref, do0_ref, do1_ref, do2_ref, do3_ref, out_ref):
     refs = (do0_ref, do1_ref, do2_ref, do3_ref)
 
-    @pl.loop(0, QT, unroll=4)
+    @pl.loop(0, QT, unroll=8)
     def _(n):
         total = st_ref[n, 1:2, :]
         some = total > 0.0
@@ -155,7 +155,7 @@
 def scale_kernel(st0_ref, st1_ref, st2_ref, st3_ref, st_ref, ot_ref, stat_ref, *out_refs):
     refs = (st0_ref, st1_ref, st2_ref, st3_ref)
 
-    @pl.loop(0, QT, unroll=4)
+    @pl.loop(0, QT, unroll=8)
     def _(n):
         parts = [refs[0][n]] + [pltpu.roll(refs[k][n], 64 * k, 1) for k in (1, 2, 3)]
         top = jnp.maximum(jnp.maximum(parts[0][0:1], parts[1][0:1]), jnp.maximum(parts[2][0:1], parts[3][0:1]))
@@ -202,13 +202,13 @@
     run(0)
     run(1)
 
-    @pl.loop(0, QT, unroll=4)
+    @pl.loop(0, QT, unroll=8)
     def _(n):
         qb = (dq[n] * SCALE).astype(bf16).T
         for h in range(4):
             out_ref[:, n, :, 640 + h * HD:768 + h * HD] = qb[h * 64:(h + 1) * 64].reshape(4, 16, HD)
 
-    @pl.loop(0, KP, unroll=4)
+    @pl.loop(0, KP, unroll=8)
     def _(p):
         for first, tile in ((0, (dk[p] * SCALE).astype(bf16)), (HD, dv[p].astype(bf16))):
             for h in (0, 1):
@@ -250,7 +250,7 @@
 
 
 def turn_kernel(own_ref, oth_ref, kt):
-    @pl.loop(0, KP, unroll=4)
+    @pl.loop(0, KP, unroll=8)
     def _(p):
         kt[:, pl.ds(pl.multiple_of(p * 256, 256), 256)] = key_tile(own_ref, oth_ref, p, 0).T
 

time: 142 us -> 144 us (1.014); the launches traced: 140 us -> 144 us
  Pallas kernels: 36.8 us -> 41 us
  waiting for transfers between devices: 33.4 us -> 31.8 us
    pallas_call x1, Pallas kernels: 18.9 us -> 21.8 us  [bwd(): pl.pallas_call(bwd_kernel, in_specs=[SMEM] + [VMEM] * 10, out_specs=[VMEM...]
    pallas_call x1, Pallas kernels: 11.5 us -> 13.2 us  [fwd(): pl.pallas_call(fwd_kernel, in_specs=[SMEM] + [VMEM] * 4, out_specs=[VMEM,...]
    ppermute x9, waiting for transfers between devices: 6.27 us -> 4.63 us  [along(): return lax.ppermute(x, 'head', [(i, (i + k) % 4) for i in range(4)])]
  transfers between devices with their start and end apart: 12 -> 12, of which waited for: 6 -> 5; matrix products, arithmetic and copies ran while one was open for 4% -> 4% of each run, Pallas kernels for 22% -> 25%
where the time goes in v2:
time: 144 us
  Pallas kernels  41 us (28%)
  blocking collectives  40.9 us (28%)
  waiting for transfers between devices  31.8 us (22%)
  starting transfers between devices  21.1 us (15%)
  other arithmetic  4.24 us (3%)
  between operations  3.61 us (3%)
    all_to_all x1, blocking collectives, on_device(): out = lax.all_to_all(out.reshape(64, 16, WIDE), PLANE, 0, 0, tiled=True)  40.9 us
    all_to_all x1, waiting for transfers between devices, on_device(): lax.all_to_all(pieces.reshape(64, 16, WIDE), PLANE, 0, 0, tiled=True)  24.5 us
    pallas_call x1, Pallas kernels, bwd(): pl.pallas_call(bwd_kernel, in_specs=[SMEM] + [VMEM] * 10, out_specs=[VMEM...  21.8 us
    pallas_call x1, Pallas kernels, fwd(): pl.pallas_call(fwd_kernel, in_specs=[SMEM] + [VMEM] * 4, out_specs=[VMEM,...  13.2 us
    all_to_all x1, starting transfers between devices, on_device(): lax.all_to_all(pieces.reshape(64, 16, WIDE), PLANE, 0, 0, tiled=True)  11.5 us
    ppermute x9, starting transfers between devices, along(): return lax.ppermute(x, 'head', [(i, (i + k) % 4) for i in range(4)])  9.38 us
    ppermute x9, waiting for transfers between devices, along(): return lax.ppermute(x, 'head', [(i, (i + k) % 4) for i in range(4)])  4.63 us
  transfers between devices with their start and end apart: 12, of which 5 were waited for; matrix products, arithmetic and copies ran while one was open for 4% of the time, Pallas kernels for 25%

profile of v2, /device:TPU:0, one launch (start us, length us, event | category | flops | bytes accessed | tf_op | source)
XLA Modules:
  0.0 143.7 jit_solution(8014613894741672530)
XLA Ops:
  0.6 2.7 %pack.1 = bf16[4,16,16,1152]{3,2,1,0:T(8,128)(2,1)} custom-call(bf16[128,1024]{1,0:T(8,128)(2,1)} %bitcast.20, bf16[128,256]{1,0:T(8,128)(2,1)} %bitcast.22, bf16[128,256]{1,0:T(8,128)(2,1)} %bitcast.23, bf16[128,1024]{1,0:T(8,128)(2,1)} %bitcast.21), custom_call_target="tpu_custom_call" | custom-call | tf_op jit(solution)/shard_map/pack/pallas_call | solution.py:312
  3.3 0.0 copy-start
  3.3 11.5 %all-to-all-start = ((bf16[64,16,1152]{2,1,0:T(8,128)(2,1)}), bf16[64,16,1152]{2,1,0:T(8,128)(2,1)S(1)}, u32[]{:S(2)}, u32[]{:S(2)}) async-start(bf16[64,16,1152]{2,1,0:T(8,128)(2,1)} %bitcast.19), calls=%async_computation | async-start | bytes 4718592 | tf_op jit(solution)/shard_map/all_to_all | solution.py:423
  14.9 0.0 copy-done
  14.9 0.1 select_reduce_fusion.3
  15.0 0.1 add.208
  15.1 0.1 add_add_fusion
  15.1 0.1 add.205
  15.2 0.1 add.206
  15.3 0.1 select_reduce_fusion.2
  15.4 0.2 fusion.4
  15.7 0.7 convert_reduce_fusion.2
  17.7 0.1 and.273
  17.7 0.1 and.274
  17.8 0.1 sub.135
  19.2 0.1 ge.113
  19.3 0.1 and.272
  19.4 0.1 tile.18
  19.5 0.1 tile.16
  19.7 0.1 convert_reduce_fusion.1
  19.8 0.6 convert_reduce_fusion.4
  20.4 0.6 convert_reduce_fusion.3
  21.1 0.1 convert_reduce_fusion
  21.2 0.2 select_reduce_fusion.1
  21.4 0.7 compare_select_fusion.1
  22.0 0.7 compare_select_fusion
  22.8 24.5 %all-to-all-done = bf16[64,16,1152]{2,1,0:T(8,128)(2,1)S(1)} async-done(((bf16[64,16,1152]{2,1,0:T(8,128)(2,1)}), bf16[64,16,1152]{2,1,0:T(8,128)(2,1)S(1)}, u32[]{:S(2)}, u32[]{:S(2)}) %all-to-all-start) | async-done | bytes 2359328 | tf_op jit(solution)/shard_map/all_to_all | solution.py:423
  47.2 0.1 broadcast_in_dim.85.kpos_ref
  47.3 0.1 slice.14
  47.5 0.1 collective-permute-start
  47.6 1.2 collective-permute-start.3
  48.8 1.0 collective-permute-start.2
  49.7 0.5 collective-permute-start.1
  50.3 0.0 collective-permute-done.oth_ref
  50.3 13.2 %fwd.1 = (f32[17,128,256]{2,1,0:T(8,128)S(1)}, f32[16,4,256]{2,1,0:T(4,128)S(1)}) custom-call(s32[2,160]{1,0:T(2,128)S(1)} %pad_add_fusion.1.steps, s32[17,2,256]{2,1,0:T(2,128)S(1)} %pad_add_fusion.pos_ref, s32[256,128]{1,0:T(8,128)S(1)} %broadcast_in_dim.85.kpos_ref, bf16[4,16,16,1152]{3,2,1,0:T(8,128)(2,1)S(1)} %bitcast.15, ...), custom_call_target="tpu_custom_call" | custom-call | flops 15000000512 | bytes 8388608 | tf_op jit(solution)/shard_map/fwd/pallas_call | solution.py:221
  63.5 0.0 collective-permute-done.3.do3_ref
  63.5 0.0 collective-permute-done.2.do2_ref
  63.5 0.8 collective-permute-done.1.do1_ref
  64.3 0.4 delta.1.st0_ref
  64.8 2.0 %collective-permute-start.6 = (f32[16,2,256]{2,1,0:T(2,128)S(1)}, f32[16,2,256]{2,1,0:T(2,128)S(1)}, u32[]{:S(2)}, u32[]{:S(2)}) collective-permute-start(f32[16,2,256]{2,1,0:T(2,128)S(1)} %delta.1.st0_ref), channel_id=1, source_target_pairs={{0,96},{32,0},{64,32},{96,64},{1,97},{33,1},{65,33},{97,65},{2,98}... | collective-permute-start | bytes 98312 | tf_op jit(solution)/shard_map/ppermute | solution.py:428
  66.7 1.4 collective-permute-start.5
  68.1 0.9 collective-permute-start.4
  69.0 0.4 turn_keys.1.kt
  69.4 0.0 collective-permute-done.6.st3_ref
  69.4 2.7 %collective-permute-done.5.st2_ref = f32[16,2,256]{2,1,0:T(2,128)S(1)} collective-permute-done((f32[16,2,256]{2,1,0:T(2,128)S(1)}, f32[16,2,256]{2,1,0:T(2,128)S(1)}, u32[]{:S(2)}, u32[]{:S(2)}) %collective-permute-start.5) | collective-permute-done | bytes 32800 | tf_op jit(solution)/shard_map/ppermute | solution.py:428
  72.1 1.1 collective-permute-done.4.st1_ref
  73.2 0.8 scale.1
  74.0 0.4 collective-permute-start.7
  74.5 1.4 collective-permute-start.8
  75.9 0.6 collective-permute-start.9
  76.5 21.8 %bwd.1 = (bf16[4,16,16,1152]{3,2,1,0:T(8,128)(2,1)S(1)}, bf16[4,16,16,512]{3,2,1,0:T(8,128)(2,1)S(1)}) custom-call(s32[2,160]{1,0:T(2,128)S(1)} %pad_add_fusion.1.steps, s32[17,2,256]{2,1,0:T(2,128)S(1)} %pad_add_fusion.pos_ref, s32[256,128]{1,0:T(8,128)S(1)} %broadcast_in_dim.85.kpos_ref, f32[17,2,256]{2,1,0:T(2,128)S(1)} %get-tuple-element.29.stat_ref, ...), custom_call_target="tpu_custom_call" | custom-call | flops 24999999488 | bytes 8388608 | tf_op jit(solution)/shard_map/bwd/pallas_call | solution.py:267
  98.3 0.0 collective-permute-done.7.o1_ref
  98.3 0.0 collective-permute-done.8.o2_ref
  98.4 0.0 collective-permute-done.9.o3_ref
  98.4 0.2 gather_parts.1
  98.6 0.1 collective-permute-start.10
  98.7 2.6 %collective-permute-done.10.other_ref = bf16[4,16,16,512]{3,2,1,0:T(8,128)(2,1)S(1)} collective-permute-done((bf16[4,16,16,512]{3,2,1,0:T(8,128)(2,1)S(1)}, bf16[4,16,16,512]{3,2,1,0:T(8,128)(2,1)S(1)}, u32[]{:S(2)}, u32[]{:S(2)}) %collective-permute-start.10) | collective-permute-done | bytes 1048608 | tf_op jit(solution)/shard_map/ppermute | solution.py:442
  101.3 0.5 add_parts.1
  101.9 40.9 %all_to_all.10.in_ref = bf16[64,16,1152]{2,1,0:T(8,128)(2,1)S(1)} all-to-all(bf16[64,16,1152]{2,1,0:T(8,128)(2,1)S(1)} %bitcast.18), channel_id=1, replica_groups=mesh['head'=4,'inner'=8,'zl'=2,'core'=2] {'head','inner','zl'}, dimensions={0} | all-to-all | bytes 4718592 | tf_op jit(solution)/shard_map/all_to_all | solution.py:443
  142.8 1.0 sum_pieces.1
  (19 shorter events, 0.2 us)
Async XLA Ops:
  3.3 11.6 %copy-start = (s32[4]{0:T(128)S(1)}, s32[4]{0:T(128)}, u32[]{:S(2)}) copy-start(s32[4]{0:T(128)} %param.9) | copy-start | bytes 52
  3.3 43.9 %all-to-all-start = ((bf16[64,16,1152]{2,1,0:T(8,128)(2,1)}), bf16[64,16,1152]{2,1,0:T(8,128)(2,1)S(1)}, u32[]{:S(2)}, u32[]{:S(2)}) async-start(bf16[64,16,1152]{2,1,0:T(8,128)(2,1)} %bitcast.19), calls=%async_computation | async-start | bytes 4718592 | tf_op jit(solution)/shard_map/all_to_all | solution.py:423
  47.5 2.8 %collective-permute-start = (bf16[4,16,16,512]{3,2,1,0:T(8,128)(2,1)S(1)}, bf16[4,16,16,512]{3,2,1,0:T(8,128)(2,1)S(1)}, u32[]{:S(2)}, u32[]{:S(2)}) collective-permute-start(bf16[4,16,16,512]{3,2,1,0:T(8,128)(2,1)S(1)} %slice.14), channel_id=1, source_target_pairs={{0,1},{1,0},{2,3},{3,2},{4,5},{5,4},{6,7},{7,6},{8,9},{9,8},{10,11... | collective-permute-start | bytes 3145736 | tf_op jit(solution)/shard_map/ppermute | solution.py:425
  47.6 15.9 %collective-permute-start.3 = (bf16[4,16,16,128]{3,2,1,0:T(8,128)(2,1)S(1)}, bf16[4,16,16,128]{3,2,1,0:T(8,128)(2,1)S(1)}, u32[]{:S(2)}, u32[]{:S(2)}) collective-permute-start(bf16[4,16,16,128]{3,2,1,0:T(8,128)(2,1)S(1)} %slice.15.do0_ref), channel_id=1, source_target_pairs={{0,96},{32,0},{64,32},{96,64},{1,97},{33,1},{65,33},{97,65},{2,98}... | collective-permute-start | bytes 786440 | tf_op jit(solution)/shard_map/ppermute | solution.py:428
  48.8 14.7 %collective-permute-start.2 = (bf16[4,16,16,128]{3,2,1,0:T(8,128)(2,1)S(1)}, bf16[4,16,16,128]{3,2,1,0:T(8,128)(2,1)S(1)}, u32[]{:S(2)}, u32[]{:S(2)}) collective-permute-start(bf16[4,16,16,128]{3,2,1,0:T(8,128)(2,1)S(1)} %slice.15.do0_ref), channel_id=1, source_target_pairs={{0,64},{32,96},{64,0},{96,32},{1,65},{33,97},{65,1},{97,33},{2,66}... | collective-permute-start | bytes 786440 | tf_op jit(solution)/shard_map/ppermute | solution.py:428
  49.7 14.6 %collective-permute-start.1 = (bf16[4,16,16,128]{3,2,1,0:T(8,128)(2,1)S(1)}, bf16[4,16,16,128]{3,2,1,0:T(8,128)(2,1)S(1)}, u32[]{:S(2)}, u32[]{:S(2)}) collective-permute-start(bf16[4,16,16,128]{3,2,1,0:T(8,128)(2,1)S(1)} %slice.15.do0_ref), channel_id=1, source_target_pairs={{0,32},{32,64},{64,96},{96,0},{1,33},{33,65},{65,97},{97,1},{2,34}... | collective-permute-start | bytes 786440 | tf_op jit(solution)/shard_map/ppermute | solution.py:428
  64.8 4.6 %collective-permute-start.6 = (f32[16,2,256]{2,1,0:T(2,128)S(1)}, f32[16,2,256]{2,1,0:T(2,128)S(1)}, u32[]{:S(2)}, u32[]{:S(2)}) collective-permute-start(f32[16,2,256]{2,1,0:T(2,128)S(1)} %delta.1.st0_ref), channel_id=1, source_target_pairs={{0,96},{32,0},{64,32},{96,64},{1,97},{33,1},{65,33},{97,65},{2,98}... | collective-permute-start | bytes 98312 | tf_op jit(solution)/shard_map/ppermute | solution.py:428
  66.7 5.4 %collective-permute-start.5 = (f32[16,2,256]{2,1,0:T(2,128)S(1)}, f32[16,2,256]{2,1,0:T(2,128)S(1)}, u32[]{:S(2)}, u32[]{:S(2)}) collective-permute-start(f32[16,2,256]{2,1,0:T(2,128)S(1)} %delta.1.st0_ref), channel_id=1, source_target_pairs={{0,64},{32,96},{64,0},{96,32},{1,65},{33,97},{65,1},{97,33},{2,66}... | collective-permute-start | bytes 98312 | tf_op jit(solution)/shard_map/ppermute | solution.py:428
  68.1 5.1 %collective-permute-start.4 = (f32[16,2,256]{2,1,0:T(2,128)S(1)}, f32[16,2,256]{2,1,0:T(2,128)S(1)}, u32[]{:S(2)}, u32[]{:S(2)}) collective-permute-start(f32[16,2,256]{2,1,0:T(2,128)S(1)} %delta.1.st0_ref), channel_id=1, source_target_pairs={{0,32},{32,64},{64,96},{96,0},{1,33},{33,65},{65,97},{97,1},{2,34}... | collective-permute-start | bytes 98312 | tf_op jit(solution)/shard_map/ppermute | solution.py:428
  74.0 24.3 %collective-permute-start.7 = (bf16[4,16,16,128]{3,2,1,0:T(8,128)(2,1)S(1)}, bf16[4,16,16,128]{3,2,1,0:T(8,128)(2,1)S(1)}, u32[]{:S(2)}, u32[]{:S(2)}) collective-permute-start(bf16[4,16,16,128]{3,2,1,0:T(8,128)(2,1)S(1)} %get-tuple-element.33), channel_id=1, source_target_pairs={{0,96},{32,0},{64,32},{96,64},{1,97},{33,1},{65,33},{97,65},{2,98}... | collective-permute-start | bytes 786440 | tf_op jit(solution)/shard_map/ppermute | solution.py:428
  74.5 23.9 %collective-permute-start.8 = (bf16[4,16,16,128]{3,2,1,0:T(8,128)(2,1)S(1)}, bf16[4,16,16,128]{3,2,1,0:T(8,128)(2,1)S(1)}, u32[]{:S(2)}, u32[]{:S(2)}) collective-permute-start(bf16[4,16,16,128]{3,2,1,0:T(8,128)(2,1)S(1)} %get-tuple-element.34), channel_id=1, source_target_pairs={{0,64},{32,96},{64,0},{96,32},{1,65},{33,97},{65,1},{97,33},{2,66}... | collective-permute-start | bytes 786440 | tf_op jit(solution)/shard_map/ppermute | solution.py:428
  75.9 22.5 %collective-permute-start.9 = (bf16[4,16,16,128]{3,2,1,0:T(8,128)(2,1)S(1)}, bf16[4,16,16,128]{3,2,1,0:T(8,128)(2,1)S(1)}, u32[]{:S(2)}, u32[]{:S(2)}) collective-permute-start(bf16[4,16,16,128]{3,2,1,0:T(8,128)(2,1)S(1)} %get-tuple-element.35), channel_id=1, source_target_pairs={{0,32},{32,64},{64,96},{96,0},{1,33},{33,65},{65,97},{97,1},{2,34}... | collective-permute-start | bytes 786440 | tf_op jit(solution)/shard_map/ppermute | solution.py:428
  98.6 2.7 %collective-permute-start.10 = (bf16[4,16,16,512]{3,2,1,0:T(8,128)(2,1)S(1)}, bf16[4,16,16,512]{3,2,1,0:T(8,128)(2,1)S(1)}, u32[]{:S(2)}, u32[]{:S(2)}) collective-permute-start(bf16[4,16,16,512]{3,2,1,0:T(8,128)(2,1)S(1)} %get-tuple-element.36), channel_id=1, source_target_pairs={{0,1},{1,0},{2,3},{3,2},{4,5},{5,4},{6,7},{7,6},{8,9},{9,8},{10,11... | collective-permute-start | bytes 3145736 | tf_op jit(solution)/shard_map/ppermute | solution.py:442
